TPU v7x, 128 devices: a whole 4x4x4 slice. The times are simulated.
128 devices in a mesh: dp: 4 (over x), section: 4 (over y_hi, core), expert: 8 (over y_lo, z).
Axes of the slice: x: 4, y: 4 (y_hi: 2, y_lo: 2; y = y_hi * 2 + y_lo), z: 4, core: 2. Of those that a mesh axis runs over, the one named last changes fastest.
Arguments:
- tokens: bfloat16 [8192, 4096], P(('dp', 'section')), may hold values from -90 to 90
- w_query: bfloat16 [4096, 2048], P(None, 'expert'), may hold values from -0.09375 to 0.09375
- w_key: bfloat16 [4096, 1024], P(None, 'expert'), may hold values from -0.09375 to 0.09375
- w_value: bfloat16 [4096, 1024], P(None, 'expert'), may hold values from -0.09375 to 0.09375
- w_out: bfloat16 [2048, 4096], P('expert'), may hold values from -0.125 to 0.125
- w_gate: bfloat16 [8, 7168, 4096], P('expert', ('dp', 'section')), may hold values from -0.09375 to 0.09375
- w_up: bfloat16 [8, 7168, 4096], P('expert', ('dp', 'section')), may hold values from -0.09375 to 0.09375
- w_down: bfloat16 [8, 7168, 4096], P('expert', ('dp', 'section')), may hold values from -0.0625 to 0.0625
- route: int32 [128, 1], P(('dp', 'section')), may hold values from 0 to 7; in each aligned block of 8 rows (0 to 7, 8 to 15, ...) at most 2 rows name the same one
- old_out: bfloat16 [128, 64, 4096], P(('dp', 'section'), 'expert'), may hold values from -6 to 6
- cotangent: bfloat16 [8192, 4096], P(('dp', 'section')), may hold values from -6 to 6
Outputs:
- joined: bfloat16 [128, 64, 4096], P(('dp', 'section'), 'expert')
- divergence: float32 [128, 64], P(('dp', 'section'), 'expert')
- grad_out_t: float32 [4096, 2048], P(('dp', 'section'), 'expert')
Inputs may be any that keep to these rules, and one draw needn't show every extreme that they name: `route`: blocks routed to experts 6 and above go to new experts. Among the 8 blocks of one replica no expert is named more than 2 times, and some replica names one expert exactly 2 times in every draw.
All inputs are finite; a program needn't handle non-finite values.
Results may differ from a plain program's by a relative error of at most 0.025.
Values may be sent and summed in bfloat16 or wider, within the bound.
No kernel may reach another device: no remote copies, remote signals or barrier semaphores. Data moves between devices by JAX's collectives and lax.ppermute only.
A program may use at most 192 MiB of HBM per device.

v0:
```python
import math
import jax
import jax.numpy as jnp
from jax import lax
from jax.sharding import PartitionSpec as P

D = 4096
HEAD_DIM = 128
BLOCK = 64


def in_blocks(value, dim, length):
    shape = value.shape
    parts = value.reshape(*shape[:dim], length, shape[dim] // length, *shape[dim + 1 :])
    return jnp.moveaxis(parts, dim, 0)


def sum_at_owner(value, axis, dim):
    parts = in_blocks(value, dim, lax.axis_size(axis))
    arrived = lax.all_to_all(parts, axis, split_axis=0, concat_axis=0, tiled=True)
    return arrived.astype(jnp.float32).sum(axis=0)


def attend_local(tokens, w_query, w_key, w_value):
    length = tokens.shape[0]
    key_heads = w_key.shape[1] // HEAD_DIM
    group = w_query.shape[1] // w_key.shape[1]
    queries = jnp.dot(tokens, w_query, preferred_element_type=jnp.float32).astype(jnp.bfloat16)
    queries = queries.reshape(length, key_heads, group, HEAD_DIM)
    keys = jnp.dot(tokens, w_key, preferred_element_type=jnp.float32).astype(jnp.bfloat16)
    keys = keys.reshape(length, key_heads, HEAD_DIM)
    values = jnp.dot(tokens, w_value, preferred_element_type=jnp.float32).astype(jnp.bfloat16)
    values = values.reshape(length, key_heads, HEAD_DIM)
    height = min(length, 512)

    def one_block(number):
        first = number * height
        scores = jnp.einsum("qkgd,skd->kgqs", queries, keys, preferred_element_type=jnp.float32)
        scores = scores * (1.0 / math.sqrt(HEAD_DIM))
        query_pos = first + lax.broadcasted_iota(jnp.int32, (height, length), 0)
        key_pos = lax.broadcasted_iota(jnp.int32, (height, length), 1)
        scores = jnp.where(query_pos >= key_pos, scores, -jnp.inf)
        top = jnp.max(scores, axis=-1, keepdims=True)
        weights = jnp.exp(scores - top)
        probs = (weights / jnp.sum(weights, axis=-1, keepdims=True)).astype(jnp.bfloat16)
        mixed = jnp.einsum("kgqs,skd->qkgd", probs, values, preferred_element_type=jnp.float32)
        return mixed.astype(jnp.bfloat16)

    mixed = lax.map(one_block, jnp.arange(length // height, dtype=jnp.int32))
    return mixed.reshape(length, key_heads * group * HEAD_DIM)


def routing_table(routes, experts, capacity):
    number = routes.shape[0]
    same = routes[:, None] == routes[None, :]
    earlier = lax.broadcasted_iota(jnp.int32, (number, number), 1) < lax.broadcasted_iota(
        jnp.int32, (number, number), 0
    )
    slot = jnp.sum((same & earlier).astype(jnp.int32), axis=1)
    expert_hit = routes[None, :] == lax.broadcasted_iota(jnp.int32, (experts, number), 0)
    slot_hit = slot[None, :] == lax.broadcasted_iota(jnp.int32, (capacity, number), 0)
    return (expert_hit[:, None, :] & slot_hit[None, :, :]).astype(jnp.bfloat16)


def wo_gradient(cotangent, heads_out):
    return sum_at_owner(
        lax.dot_general(
            cotangent, heads_out, (((0,), (0,)), ((), ())), preferred_element_type=jnp.float32
        ).astype(jnp.bfloat16),
        ("dp", "section"),
        0,
    )


def per_device(
    tokens, w_query, w_key, w_value, w_out, w_gate, w_up, w_down, route, old_out, cotangent
):
    experts = lax.axis_size("expert")
    own_index = lax.axis_index("expert")
    length = tokens.shape[0]
    blocks = length // BLOCK
    piece_rows = BLOCK // experts
    capacity = max(2, blocks // experts + 1)
    old_count = experts - max(1, experts // 4)
    routes = route[:, 0]
    table = routing_table(routes, experts, capacity)
    heads_out = attend_local(tokens, w_query, w_key, w_value)
    partial_value = jnp.dot(heads_out, w_out, preferred_element_type=jnp.float32).reshape(
        blocks, BLOCK, D
    )
    token_blocks = tokens.reshape(blocks, BLOCK, D)
    attention = lax.psum_scatter(
        partial_value.astype(jnp.bfloat16), "expert", scatter_dimension=1, tiled=True
    ).astype(jnp.float32)
    own_rows = lax.dynamic_slice_in_dim(token_blocks, own_index * piece_rows, piece_rows, 1)
    hidden_in = (own_rows.astype(jnp.float32) + attention).astype(jnp.bfloat16)
    outgoing = jnp.einsum(
        "jcb,brd->jcrd", table, hidden_in, preferred_element_type=jnp.float32
    ).astype(jnp.bfloat16)
    arrived = lax.all_to_all(outgoing, "expert", split_axis=0, concat_axis=0, tiled=True)
    expert_rows = arrived.reshape(experts * capacity * piece_rows, D)
    gate_rows = w_gate[0]
    up_rows = w_up[0]
    down_rows = w_down[0]
    contract = (((1,), (1,)), ((), ()))
    piece = lax.all_gather(expert_rows, ("dp", "section"), axis=0, tiled=True)
    gate = lax.dot_general(piece, gate_rows, contract, preferred_element_type=jnp.float32)
    lifted = lax.dot_general(piece, up_rows, contract, preferred_element_type=jnp.float32)
    active = (jax.nn.silu(gate) * lifted).astype(jnp.bfloat16)
    expert_sum = lax.psum_scatter(
        jnp.dot(active, down_rows, preferred_element_type=jnp.float32).astype(jnp.bfloat16),
        ("dp", "section"),
        scatter_dimension=0,
        tiled=True,
    )
    returned = lax.all_to_all(
        expert_sum.reshape(experts, capacity, piece_rows, D),
        "expert",
        split_axis=0,
        concat_axis=0,
        tiled=True,
    )
    merged = jnp.einsum("jcb,jcrd->brd", table, returned, preferred_element_type=jnp.float32)
    joined = (hidden_in.astype(jnp.float32) + merged).astype(jnp.bfloat16)
    fresh = (routes >= old_count).astype(jnp.float32)
    gap = joined.astype(jnp.float32) - old_out.astype(jnp.float32)
    divergence = 0.5 * jnp.mean(gap * gap, axis=-1) * fresh[:, None]
    gradient = wo_gradient(cotangent, heads_out)
    return (joined, divergence, gradient)


def solution(mesh):
    return jax.shard_map(
        per_device,
        mesh=mesh,
        in_specs=(
            P(("dp", "section"), None),
            P(None, "expert"),
            P(None, "expert"),
            P(None, "expert"),
            P("expert", None),
            P("expert", ("dp", "section"), None),
            P("expert", ("dp", "section"), None),
            P("expert", ("dp", "section"), None),
            P(("dp", "section"), None),
            P(("dp", "section"), "expert", None),
            P(("dp", "section"), None),
        ),
        out_specs=(
            P(("dp", "section"), "expert", None),
            P(("dp", "section"), "expert"),
            P(("dp", "section"), "expert"),
        ),
        check_vma=False,
    )
```

profile of v0, /device:TPU:1, one launch (start us, length us, event | category | flops | bytes accessed | tf_op | source)
XLA Modules:
  0.0 434.4 jit_solution(16842746482815868025)
XLA Ops:
  7.2 0.0 copy-start
  7.2 0.0 reduce-scatter.7.cloned.1.call-start
  7.2 0.1 iota_compare_fusion
  7.3 0.0 copy-start.3
  7.3 5.0 %convolution_convert_fusion.5 = bf16[512,256]{0,1:T(8,128)(2,1)} fusion(bf16[512,4096]{1,0:T(8,128)(2,1)} %param.11, bf16[4096,256]{1,0:T(8,128)(2,1)} %param.12), kind=kOutput, calls=%fused_computation.22 | convolution fusion | flops 1073872896 | bytes 6553600 | tf_op jit(solution)/shard_map/dot_general | solution.py:28
  12.3 0.0 copy-done.3
  12.3 5.6 %fusion.27 = (f32[2,512]{1,0:T(2,128)S(1)}, f32[1,2,512,512]{2,3,1,0:T(8,128)}) fusion(bf16[512,2,128]{0,2,1:T(8,128)(2,1)} %bitcast.121, bf16[512,4096]{1,0:T(8,128)(2,1)} %param.11, bf16[4096,128]{1,0:T(8,128)(2,1)S(1)} %copy-done.3, pred[512,512]{0,1:T(8,128)(4,1)S(1)} %iota_compare_fusion), kind=kOutput, calls=%fused_computation.51 | convolution fusion | flops 672726016 | bytes 7868416 | tf_op jit(solution)/shard_map/while/body/eval_jaxpr/qkgd,skd->kgqs/dot_general | solution.py:38
  18.0 1.9 fusion.12
  19.9 4.9 %convolution_convert_fusion.4 = bf16[128,2,512]{2,0,1:T(8,128)(2,1)S(1)} fusion(bf16[512,4096]{1,0:T(8,128)(2,1)} %param.11, bf16[4096,128]{1,0:T(8,128)(2,1)} %param.14, f32[1,2,512,512]{2,3,1,0:T(8,128)} %get-tuple-element.28, f32[2,512]{1,0:T(2,128)S(1)} %fusion.12, f32[2,512]{1,0:T(2,128)S(1)} %get-tuple-element.27), kind=kOutput, calls=%fused_computation.21 | convolution fusion | flops 672858112 | bytes 7610368 | tf_op jit(solution)/shard_map/while/body/eval_jaxpr/kgqs,skd->qkgd/dot_general | solution.py:46
  24.8 0.2 copy.62
  24.9 0.2 dot_general.45
  25.1 0.0 copy-done
  25.1 1.3 fusion.28
  26.4 2.2 copy.87
  28.6 0.0 copy-start.4
  28.6 0.0 reduce-scatter.7.cloned.1.call-update
  28.6 0.0 all-gather.2.cloned.1.call-start
  28.7 0.6 copy-done.4
  29.3 0.1 convert_reduce_fusion.1
  29.4 0.1 iota_compare_fusion.2
  29.4 1.1 constant_dynamic-slice_fusion
  30.5 54.8 %reduce-scatter.7.cloned.1.call-done = bf16[8,32768]{1,0:T(8,128)(2,1)} async-done(((bf16[64,32768]{1,0:T(8,128)(2,1)}), bf16[8,32768]{1,0:T(8,128)(2,1)}) %reduce-scatter.7.cloned.1.call-update) | async-done | bytes 524304
  85.3 2.3 convolution_convert_fusion.3
  87.7 0.6 copy.65
  88.3 17.5 %all_to_all.15 = bf16[8,2,8,4096]{3,2,1,0:T(8,128)(2,1)} all-to-all(bf16[8,2,8,4096]{3,2,1,0:T(8,128)(2,1)S(1)} %copy.65), channel_id=1, replica_groups=mesh['dp'=4,'section'=4,'expert'=8] {'expert'}, dimensions={0} | all-to-all | bytes 2097152 | tf_op jit(solution)/shard_map/all_to_all | solution.py:100
  105.8 0.0 all-gather.2.cloned.1.call-update
  105.8 0.2 reduce-scatter.5.cloned.1.call-start
  106.0 110.8 %all-gather.2.cloned.1.call-done = bf16[2048,4096]{1,0:T(8,128)(2,1)} async-done(((bf16[128,4096]{1,0:T(8,128)(2,1)}), bf16[2048,4096]{1,0:T(8,128)(2,1)}) %all-gather.2.cloned.1.call-update) | async-done | bytes 16777232 | tf_op jit(solution)/shard_map/all_gather | solution.py:106
  216.8 13.7 %fusion.5 = f32[2048,448]{0,1:T(8,128)} fusion(bf16[2048,4096]{1,0:T(8,128)(2,1)} %all-gather.2.cloned.1.call-done, bf16[1,448,4096]{2,1,0:T(8,128)(2,1)} %param.16), kind=kOutput, calls=%fused_computation.11 | convolution fusion | flops 7516192768 | bytes 24117248 | tf_op jit(solution)/shard_map/dot_general | solution.py:107
  230.5 24.4 %convolution_convert_fusion = bf16[2048,4096]{1,0:T(8,128)(2,1)} fusion(bf16[1,448,4096]{2,1,0:T(8,128)(2,1)} %param.18, f32[2048,448]{0,1:T(8,128)} %fusion.5, bf16[2048,4096]{1,0:T(8,128)(2,1)} %all-gather.2.cloned.1.call-done, bf16[1,448,4096]{2,1,0:T(8,128)(2,1)} %param.17), kind=kOutput, calls=%fused_computation | convolution fusion | flops 15046279168 | bytes 44564480 | tf_op jit(solution)/shard_map/dot_general | solution.py:111
  254.9 0.0 reduce-scatter.5.cloned.1.call-update
  254.9 3.4 convolution_convert_fusion.2
  258.3 1.5 copy.108
  259.9 4.4 %all-to-all-start.2 = ((bf16[16,256,256]{1,2,0:T(8,128)(2,1)}), bf16[16,256,256]{1,2,0:T(8,128)(2,1)}, u32[]{:S(2)}, u32[]{:S(2)}) async-start(bf16[16,256,256]{1,2,0:T(8,128)(2,1)} %bitcast.109), calls=%async_computation.3 | async-start | bytes 4194304 | tf_op jit(solution)/shard_map/all_to_all | solution.py:20
  264.3 0.0 copy-start.2
  264.3 135.2 %reduce-scatter.5.cloned.1.call-done = bf16[128,4096]{1,0:T(8,128)(2,1)} async-done(((bf16[2048,4096]{1,0:T(8,128)(2,1)}), bf16[128,4096]{1,0:T(8,128)(2,1)}) %reduce-scatter.5.cloned.1.call-update) | async-done | bytes 1048592 | tf_op jit(solution)/shard_map/reduce_scatter | solution.py:110
  399.5 3.3 copy.66
  402.8 0.0 all-to-all-done.2
  402.8 4.5 %all-to-all-start.1 = ((bf16[8,2,8,4096]{3,1,2,0:T(2,128)(2,1)}), bf16[8,2,8,4096]{3,1,2,0:T(2,128)(2,1)}, u32[]{:S(2)}, u32[]{:S(2)}) async-start(bf16[8,2,8,4096]{3,1,2,0:T(2,128)(2,1)} %copy.66), calls=%async_computation.2 | async-start | bytes 2097152 | tf_op jit(solution)/shard_map/all_to_all | solution.py:116
  407.2 0.0 copy-start.1
  407.3 2.0 convert_reduce_fusion
  409.3 0.8 copy.73
  410.2 12.2 %all-to-all-done.1 = bf16[8,2,8,4096]{3,1,2,0:T(2,128)(2,1)} async-done(((bf16[8,2,8,4096]{3,1,2,0:T(2,128)(2,1)}), bf16[8,2,8,4096]{3,1,2,0:T(2,128)(2,1)}, u32[]{:S(2)}, u32[]{:S(2)}) %all-to-all-start.1) | async-done | bytes 1048608 | tf_op jit(solution)/shard_map/all_to_all | solution.py:116
  422.3 0.0 copy-done.2
  422.3 3.7 multiply_reduce_fusion
  426.1 1.1 copy.71
  427.2 0.7 copy.72
  427.8 0.0 copy-done.1
  (3 shorter events, 0.0 us)
Async XLA Ops:
  7.2 18.0 %copy-start = (bf16[256,4096]{1,0:T(8,128)(2,1)S(1)}, bf16[256,4096]{1,0:T(8,128)(2,1)}, u32[]{:S(2)}) copy-start(bf16[256,4096]{1,0:T(8,128)(2,1)} %param.15) | copy-start | bytes 6291460
  7.2 78.2 %reduce-scatter.7.cloned.1.call-start = ((), (), s32[]{:S(2)}) async-start(), calls=%async_computation.7 | async-start | bytes 4718592
  7.3 5.0 %copy-start.3 = (bf16[4096,128]{1,0:T(8,128)(2,1)S(1)}, bf16[4096,128]{1,0:T(8,128)(2,1)}, u32[]{:S(2)}) copy-start(bf16[4096,128]{1,0:T(8,128)(2,1)} %param.13) | copy-start | bytes 3145732
  28.6 0.7 copy-start.4
  28.6 188.2 %all-gather.2.cloned.1.call-start = ((), (), s32[]{:S(2)}) async-start(), calls=%async_computation.5 | async-start | bytes 17825792 | tf_op jit(solution)/shard_map/all_gather | solution.py:106
  105.8 293.7 %reduce-scatter.5.cloned.1.call-start = ((), (), s32[]{:S(2)}) async-start(), calls=%async_computation.6 | async-start | bytes 17825792 | tf_op jit(solution)/shard_map/reduce_scatter | solution.py:110
  259.9 142.9 %all-to-all-start.2 = ((bf16[16,256,256]{1,2,0:T(8,128)(2,1)}), bf16[16,256,256]{1,2,0:T(8,128)(2,1)}, u32[]{:S(2)}, u32[]{:S(2)}) async-start(bf16[16,256,256]{1,2,0:T(8,128)(2,1)} %bitcast.109), calls=%async_computation.3 | async-start | bytes 4194304 | tf_op jit(solution)/shard_map/all_to_all | solution.py:20
  264.3 158.1 %copy-start.2 = (bf16[8,32768]{1,0:T(8,128)(2,1)S(1)}, bf16[8,32768]{1,0:T(8,128)(2,1)}, u32[]{:S(2)}) copy-start(bf16[8,32768]{1,0:T(8,128)(2,1)} %reduce-scatter.7.cloned.1.call-done) | copy-start | bytes 1572868
  402.8 19.5 %all-to-all-start.1 = ((bf16[8,2,8,4096]{3,1,2,0:T(2,128)(2,1)}), bf16[8,2,8,4096]{3,1,2,0:T(2,128)(2,1)}, u32[]{:S(2)}, u32[]{:S(2)}) async-start(bf16[8,2,8,4096]{3,1,2,0:T(2,128)(2,1)} %copy.66), calls=%async_computation.2 | async-start | bytes 2097152 | tf_op jit(solution)/shard_map/all_to_all | solution.py:116
  407.2 20.6 %copy-start.1 = (bf16[256,4096]{1,0:T(8,128)(2,1)S(1)}, bf16[256,4096]{1,0:T(8,128)(2,1)}, u32[]{:S(2)}) copy-start(bf16[256,4096]{1,0:T(8,128)(2,1)} %param.15) | copy-start | bytes 6291460
Sparse Core Ops, SparseCore 0:
  28.7 56.5 reduce-scatter.6
  105.9 110.8 all-gather.1
  255.0 144.4 reduce-scatter.4
where the time goes:
time: 435 us; the launch traced here: 434 us
  waiting for transfers between devices  313 us (72%)
  matrix products  64.4 us (15%)
  blocking collectives  17.5 us (4%)
  between operations  13.9 us (3%)
  local copies, waits for them, and re-layouts  12.2 us (3%)
  starting transfers between devices  9.16 us (2%)
    reduce_scatter x1, waiting for transfers between devices, per_device(): lax.psum_scatter(jnp.dot(active, down_rows, preferred_element_type=jnp.fl...  135 us
    all_gather x1, waiting for transfers between devices, per_device(): piece = lax.all_gather(expert_rows, ('dp', 'section'), axis=0, tiled=True)  111 us
    unnamed x4, waiting for transfers between devices  54.9 us
    dot_general x1, matrix products, per_device(): jnp.dot(active, down_rows, preferred_element_type=jnp.float32)  24.4 us
    all_to_all x1, blocking collectives, per_device(): lax.all_to_all(outgoing, 'expert', split_axis=0, concat_axis=0, tiled=True)  17.5 us
    dot_general x1, matrix products, per_device(): lax.dot_general(piece, gate_rows, contract, preferred_element_type=jnp.fl...  13.7 us
    all_to_all x1, waiting for transfers between devices, per_device(): lax.all_to_all(expert_sum.reshape(experts, capacity, piece_rows, D), 'exp...  12.2 us
  transfers between devices with their start and end apart: 5, of which 4 were waited for; matrix products, arithmetic and copies ran while one was open for 3% of the time, Pallas kernels for 0%

commit v1 on v0

--- a/solution.py
+++ b/solution.py
@@ -103,7 +103,15 @@
     up_rows = w_up[0]
     down_rows = w_down[0]
     contract = (((1,), (1,)), ((), ()))
-    piece = lax.all_gather(expert_rows, ("dp", "section"), axis=0, tiled=True)
+    piece = jnp.concatenate(
+        lax.all_to_all(
+            jnp.stack(lax.axis_size(("dp", "section")) * [expert_rows]),
+            axis_name=("dp", "section"),
+            split_axis=0,
+            concat_axis=0,
+        ),
+        0,
+    )
     gate = lax.dot_general(piece, gate_rows, contract, preferred_element_type=jnp.float32)
     lifted = lax.dot_general(piece, up_rows, contract, preferred_element_type=jnp.float32)
     active = (jax.nn.silu(gate) * lifted).astype(jnp.bfloat16)

time: 435 us -> 520 us (1.20)
  blocking collectives: 17.5 us -> 211 us
  waiting for transfers between devices: 313 us -> 200 us
  local copies, waits for them, and re-layouts: 12.2 us -> 19.9 us
    all_to_all x0 -> x1, blocking collectives: none -> 194 us  [per_device(): lax.all_to_all(jnp.stack(lax.axis_size(('dp', 'section')) * [expert_rows]...]
    all_gather x1 -> x0, waiting for transfers between devices: 111 us -> none  [per_device(): piece = lax.all_gather(expert_rows, ('dp', 'section'), axis=0, tiled=True)]
    unnamed x14 -> x18, local copies, waits for them, and re-layouts: 5.39 us -> 11.1 us
    unnamed x4 -> x3, waiting for transfers between devices: 54.9 us -> 54.9 us
  transfers between devices with their start and end apart: 5 -> 4, of which waited for: 4 -> 3; matrix products, arithmetic and copies ran while one was open for 3% -> 2% of each run, Pallas kernels for 0% -> 0%
where the time goes in v1:
time: 520 us
  blocking collectives  211 us (41%)
  waiting for transfers between devices  200 us (38%)
  matrix products  60.3 us (12%)
  local copies, waits for them, and re-layouts  19.9 us (4%)
  between operations  14.2 us (3%)
  starting transfers between devices  10.1 us (2%)
    all_to_all x1, blocking collectives, per_device(): lax.all_to_all(jnp.stack(lax.axis_size(('dp', 'section')) * [expert_rows]...  194 us
    reduce_scatter x1, waiting for transfers between devices, per_device(): lax.psum_scatter(jnp.dot(active, down_rows, preferred_element_type=jnp.fl...  134 us
    unnamed x3, waiting for transfers between devices  54.9 us
    dot_general x1, matrix products, per_device(): jnp.dot(active, down_rows, preferred_element_type=jnp.float32)  24.4 us
    all_to_all x1, blocking collectives, per_device(): lax.all_to_all(outgoing, 'expert', split_axis=0, concat_axis=0, tiled=True)  16.8 us
    all_to_all x1, waiting for transfers between devices, per_device(): lax.all_to_all(expert_sum.reshape(experts, capacity, piece_rows, D), 'exp...  11.3 us
    unnamed x18, local copies, waits for them, and re-layouts  11.1 us
  transfers between devices with their start and end apart: 4, of which 3 were waited for; matrix products, arithmetic and copies ran while one was open for 2% of the time, Pallas kernels for 0%

profile of v1, /device:TPU:1, one launch (start us, length us, event | category | flops | bytes accessed | tf_op | source)
XLA Modules:
  0.0 519.6 jit_solution(8141521332744974606)
XLA Ops:
  7.2 0.0 copy-start
  7.2 0.0 reduce-scatter.7.cloned.1.call-start
  7.2 0.1 iota_compare_fusion
  7.3 0.0 copy-start.5
  7.3 5.0 convolution_convert_fusion.5
  12.3 0.0 copy-done.5
  12.3 5.6 %fusion.27 = (f32[2,512]{1,0:T(2,128)S(1)}, f32[1,2,512,512]{2,3,1,0:T(8,128)}) fusion(bf16[512,2,128]{0,2,1:T(8,128)(2,1)} %bitcast.124, bf16[512,4096]{1,0:T(8,128)(2,1)} %param.11, bf16[4096,128]{1,0:T(8,128)(2,1)S(1)} %copy-done.5, pred[512,512]{0,1:T(8,128)(4,1)S(1)} %iota_compare_fusion), kind=kOutput, calls=%fused_computation.51 | convolution fusion | flops 672726016 | bytes 7868416 | tf_op jit(solution)/shard_map/while/body/eval_jaxpr/qkgd,skd->kgqs/dot_general | solution.py:38
  18.0 1.9 fusion.12
  19.9 4.9 convolution_convert_fusion.4
  24.8 0.2 copy.62
  24.9 0.2 dot_general.45
  25.1 0.0 copy-done
  25.1 1.3 fusion.28
  26.4 2.2 copy.87
  28.6 0.0 copy-start.6
  28.6 0.0 reduce-scatter.7.cloned.1.call-update
  28.6 0.0 reduce-scatter.5.cloned.1.call-start
  28.7 0.6 copy-done.6
  29.3 0.1 convert_reduce_fusion.1
  29.4 0.1 iota_compare_fusion.2
  29.4 1.1 constant_dynamic-slice_fusion
  30.5 54.8 %reduce-scatter.7.cloned.1.call-done = bf16[8,32768]{1,0:T(8,128)(2,1)} async-done(((bf16[64,32768]{1,0:T(8,128)(2,1)}), bf16[8,32768]{1,0:T(8,128)(2,1)}) %reduce-scatter.7.cloned.1.call-update) | async-done | bytes 524304
  85.3 2.3 convolution_convert_fusion.3
  87.7 0.6 copy.65
  88.3 16.8 %all_to_all.20 = bf16[8,2,8,4096]{3,2,1,0:T(8,128)(2,1)S(1)} all-to-all(bf16[8,2,8,4096]{3,2,1,0:T(8,128)(2,1)S(1)} %copy.65), channel_id=1, replica_groups=mesh['dp'=4,'section'=4,'expert'=8] {'expert'}, dimensions={0} | all-to-all | bytes 2097152 | tf_op jit(solution)/shard_map/all_to_all | solution.py:100
  105.1 1.9 stack.3
  107.0 0.0 copy-start.4
  107.0 194.1 %all_to_all.21 = bf16[16,128,4096]{2,1,0:T(8,128)(2,1)S(1)} all-to-all(bf16[16,128,4096]{2,1,0:T(8,128)(2,1)S(1)} %stack.3), channel_id=1, replica_groups=mesh['dp'=4,'section'=4,'expert'=8] {'dp','section'}, dimensions={0} | all-to-all | bytes 33554432 | tf_op jit(solution)/shard_map/all_to_all | solution.py:107
  301.1 0.0 copy-start.2
  301.1 5.7 %copy-done.2 = bf16[16,128,4096]{2,1,0:T(8,128)(2,1)} copy-done((bf16[16,128,4096]{2,1,0:T(8,128)(2,1)}, bf16[16,128,4096]{2,1,0:T(8,128)(2,1)S(1)}, u32[]{:S(2)}) %copy-start.2) | copy-done | bytes 16777240
  306.9 0.0 copy-done.4
  306.9 9.6 %fusion.5 = f32[2048,448]{0,1:T(8,128)} fusion(bf16[2048,4096]{1,0:T(8,128)(2,1)S(1)} %bitcast.111, bf16[1,448,4096]{2,1,0:T(8,128)(2,1)S(1)} %copy-done.4), kind=kOutput, calls=%fused_computation.11 | convolution fusion | flops 7516192768 | bytes 24117248 | tf_op jit(solution)/shard_map/dot_general | solution.py:115
  316.5 24.4 %convolution_convert_fusion = bf16[2048,4096]{1,0:T(8,128)(2,1)} fusion(bf16[1,448,4096]{2,1,0:T(8,128)(2,1)} %param.18, f32[2048,448]{0,1:T(8,128)} %fusion.5, bf16[2048,4096]{1,0:T(8,128)(2,1)} %bitcast.112, bf16[1,448,4096]{2,1,0:T(8,128)(2,1)} %param.17), kind=kOutput, calls=%fused_computation | convolution fusion | flops 15046279168 | bytes 44564480 | tf_op jit(solution)/shard_map/dot_general | solution.py:119
  340.8 0.0 reduce-scatter.5.cloned.1.call-update
  340.9 3.4 convolution_convert_fusion.2
  344.3 1.5 copy.108
  345.8 5.8 %all-to-all-start.3 = ((bf16[16,256,256]{1,2,0:T(8,128)(2,1)}), bf16[16,256,256]{1,2,0:T(8,128)(2,1)}, u32[]{:S(2)}, u32[]{:S(2)}) async-start(bf16[16,256,256]{1,2,0:T(8,128)(2,1)} %bitcast.110), calls=%async_computation.4 | async-start | bytes 4194304 | tf_op jit(solution)/shard_map/all_to_all | solution.py:20
  351.6 0.0 copy-start.3
  351.6 133.9 %reduce-scatter.5.cloned.1.call-done = bf16[128,4096]{1,0:T(8,128)(2,1)} async-done(((bf16[2048,4096]{1,0:T(8,128)(2,1)}), bf16[128,4096]{1,0:T(8,128)(2,1)}) %reduce-scatter.5.cloned.1.call-update) | async-done | bytes 1048592 | tf_op jit(solution)/shard_map/reduce_scatter | solution.py:118
  485.5 3.3 copy.66
  488.8 0.0 all-to-all-done.3
  488.8 4.2 all-to-all-start.2
  493.1 0.0 copy-start.1
  493.1 2.0 convert_reduce_fusion
  495.1 0.8 copy.73
  496.0 11.3 %all-to-all-done.2 = bf16[8,2,8,4096]{3,1,2,0:T(2,128)(2,1)} async-done(((bf16[8,2,8,4096]{3,1,2,0:T(2,128)(2,1)}), bf16[8,2,8,4096]{3,1,2,0:T(2,128)(2,1)}, u32[]{:S(2)}, u32[]{:S(2)}) %all-to-all-start.2) | async-done | bytes 1048608 | tf_op jit(solution)/shard_map/all_to_all | solution.py:124
  507.3 0.0 copy-done.3
  507.3 3.7 multiply_reduce_fusion
  511.0 1.1 copy.71
  512.1 0.7 copy.72
  512.8 0.0 copy-done.1
  (3 shorter events, 0.0 us)
Async XLA Ops:
  7.2 18.0 %copy-start = (bf16[256,4096]{1,0:T(8,128)(2,1)S(1)}, bf16[256,4096]{1,0:T(8,128)(2,1)}, u32[]{:S(2)}) copy-start(bf16[256,4096]{1,0:T(8,128)(2,1)} %param.15) | copy-start | bytes 6291460
  7.2 78.2 %reduce-scatter.7.cloned.1.call-start = ((), (), s32[]{:S(2)}) async-start(), calls=%async_computation.7 | async-start | bytes 4718592
  7.3 5.0 copy-start.5
  28.6 0.7 copy-start.6
  28.6 456.9 %reduce-scatter.5.cloned.1.call-start = ((), (), s32[]{:S(2)}) async-start(), calls=%async_computation.6 | async-start | bytes 17825792 | tf_op jit(solution)/shard_map/reduce_scatter | solution.py:118
  107.0 199.9 %copy-start.4 = (bf16[1,448,4096]{2,1,0:T(8,128)(2,1)S(1)}, bf16[1,448,4096]{2,1,0:T(8,128)(2,1)}, u32[]{:S(2)}) copy-start(bf16[1,448,4096]{2,1,0:T(8,128)(2,1)} %param.16) | copy-start | bytes 11010052
  301.1 5.7 %copy-start.2 = (bf16[16,128,4096]{2,1,0:T(8,128)(2,1)}, bf16[16,128,4096]{2,1,0:T(8,128)(2,1)S(1)}, u32[]{:S(2)}) copy-start(bf16[16,128,4096]{2,1,0:T(8,128)(2,1)S(1)} %all_to_all.21) | copy-start | bytes 50331652
  345.8 143.0 %all-to-all-start.3 = ((bf16[16,256,256]{1,2,0:T(8,128)(2,1)}), bf16[16,256,256]{1,2,0:T(8,128)(2,1)}, u32[]{:S(2)}, u32[]{:S(2)}) async-start(bf16[16,256,256]{1,2,0:T(8,128)(2,1)} %bitcast.110), calls=%async_computation.4 | async-start | bytes 4194304 | tf_op jit(solution)/shard_map/all_to_all | solution.py:20
  351.6 155.7 %copy-start.3 = (bf16[8,32768]{1,0:T(8,128)(2,1)S(1)}, bf16[8,32768]{1,0:T(8,128)(2,1)}, u32[]{:S(2)}) copy-start(bf16[8,32768]{1,0:T(8,128)(2,1)} %reduce-scatter.7.cloned.1.call-done) | copy-start | bytes 1572868
  488.8 18.5 %all-to-all-start.2 = ((bf16[8,2,8,4096]{3,1,2,0:T(2,128)(2,1)}), bf16[8,2,8,4096]{3,1,2,0:T(2,128)(2,1)}, u32[]{:S(2)}, u32[]{:S(2)}) async-start(bf16[8,2,8,4096]{3,1,2,0:T(2,128)(2,1)} %copy.66), calls=%async_computation.3 | async-start | bytes 2097152 | tf_op jit(solution)/shard_map/all_to_all | solution.py:124
  493.1 19.7 %copy-start.1 = (bf16[256,4096]{1,0:T(8,128)(2,1)S(1)}, bf16[256,4096]{1,0:T(8,128)(2,1)}, u32[]{:S(2)}) copy-start(bf16[256,4096]{1,0:T(8,128)(2,1)} %param.15) | copy-start | bytes 6291460
Sparse Core Ops, SparseCore 0:
  28.7 56.5 reduce-scatter.6
  341.0 144.4 reduce-scatter.4
